TPU v7x, 32 devices: a whole 2x2x4 slice. The times are simulated.
32 devices in a mesh: seq: 2 (over x), chan: 16 (over z, y, core).
Axes of the slice: x: 2, y: 2, z: 4, core: 2. Of those that a mesh axis runs over, the one named last changes fastest.
Arguments:
- tokens: bfloat16 [2048, 4096], P('seq', 'chan'), may hold values from -6 to 6
- in_weight: bfloat16 [4096, 3, 4096], P(None, None, 'chan'), may hold values from -0.09375 to 0.09375
- short_taps: float32 [3, 3, 4096], P(None, None, 'chan'), may hold values from -3 to 3
- filter_taps: float32 [2048, 4096], P('seq', 'chan'), may hold values from -1 to 1
- skip_gain: float32 [4096], P('chan'), may hold values from -4 to 4
- out_weight: bfloat16 [4096, 4096], P('chan'), may hold values from -0.125 to 0.125
Outputs:
- layer_out: bfloat16 [2048, 4096], P('seq', 'chan')
All inputs are finite; a program needn't handle non-finite values.
Results may differ from a plain program's by a relative error of at most 0.007.
Values may be sent and summed in bfloat16 or wider, within the bound.
A program may use at most 128 MiB of HBM per device.

v0:
```python
import math

import jax
import jax.numpy as jnp
from jax import lax
from jax.sharding import PartitionSpec as P

COLS = 256


highest = lax.Precision.HIGHEST


def from_behind(shard, axis, by):
    size = lax.axis_size(axis)
    pairs = [(i, i + by) for i in range(size) if 0 <= i + by < size]
    return lax.ppermute(shard, axis, pairs)


def phase_table(row_count, col_count, period):
    row_index = jnp.arange(row_count, dtype=jnp.int32)[:, None]
    col_index = jnp.arange(col_count, dtype=jnp.int32)[None, :]
    angle = (row_index * col_index % period).astype(jnp.float32) * (2.0 * math.pi / period)
    return (jnp.cos(angle), jnp.sin(angle))


def real_transform(signal, cosine, sines, pattern):
    real_part = jnp.einsum(pattern, cosine, signal, precision=highest)
    imag_part = -jnp.einsum(pattern, sines, signal, precision=highest)
    return (real_part, imag_part)


def complex_transform(real_part, imag_part, cosine, sines, direction, pattern):
    cos_real = jnp.einsum(pattern, cosine, real_part, precision=highest)
    cos_imag = jnp.einsum(pattern, cosine, imag_part, precision=highest)
    sin_real = jnp.einsum(pattern, sines, real_part, precision=highest)
    sin_imag = jnp.einsum(pattern, sines, imag_part, precision=highest)
    return (cos_real - direction * sin_imag, cos_imag + direction * sin_real)


def rotate(real_part, imag_part, cosine, sines, direction):
    return (
        real_part * cosine - direction * imag_part * sines,
        imag_part * cosine + direction * real_part * sines,
    )


def spectrum_product(real_part, imag_part):
    prod_real = real_part[0] * real_part[1] - imag_part[0] * imag_part[1]
    prod_imag = real_part[0] * imag_part[1] + imag_part[0] * real_part[1]
    return (prod_real[None], prod_imag[None])


def real_inverse(real_part, imag_part, cosine, sines, pattern, length):
    return (
        jnp.einsum(pattern, cosine, real_part, precision=highest)
        - jnp.einsum(pattern, sines, imag_part, precision=highest)
    ) / length


def channel_convolve(signal, filter_taps):
    stacked = jnp.stack([signal, filter_taps])
    whole_seq = lax.all_to_all(stacked, "seq", split_axis=2, concat_axis=1, tiled=True)
    length = whole_seq.shape[1]
    narrow = whole_seq.shape[2]
    full_rows = 2 * length // COLS
    half_rows = full_rows // 2
    period = 2 * length
    laid_out = whole_seq.reshape(2, half_rows, COLS, narrow)
    first_cos, first_sin = phase_table(full_rows, half_rows, full_rows)
    real_part, imag_part = real_transform(laid_out, first_cos, first_sin, "kn,xnmc->xkmc")
    twist_cos, twist_sin = phase_table(full_rows, COLS, period)
    twist_cos = twist_cos[:, :, None]
    twist_sin = twist_sin[:, :, None]
    real_part, imag_part = rotate(real_part, imag_part, twist_cos, twist_sin, -1.0)
    second_cos, second_sin = phase_table(COLS, COLS, COLS)
    pattern = "kn,xanc->xakc"
    real_part, imag_part = complex_transform(
        real_part, imag_part, second_cos, second_sin, -1.0, pattern
    )
    real_part, imag_part = spectrum_product(real_part, imag_part)
    real_part, imag_part = complex_transform(
        real_part, imag_part, second_cos, second_sin, 1.0, pattern
    )
    real_part, imag_part = rotate(real_part, imag_part, twist_cos, twist_sin, 1.0)
    last_cos, last_sin = phase_table(half_rows, full_rows, full_rows)
    values = real_inverse(real_part, imag_part, last_cos, last_sin, "nk,xkmc->xnmc", period)
    values = values.reshape(length, narrow)
    return lax.all_to_all(values, "seq", split_axis=0, concat_axis=1, tiled=True)


def body(tokens, in_weight, short_taps, filter_taps, skip_gain, out_weight):
    tok_count = tokens.shape[0]
    chan_count = in_weight.shape[2]
    flat_weight = in_weight.reshape(in_weight.shape[0], 3 * chan_count)
    projected = jnp.dot(
        lax.all_gather(tokens, "chan", axis=1, tiled=True),
        flat_weight,
        preferred_element_type=jnp.float32,
    )
    projected = projected.astype(jnp.bfloat16).reshape(tok_count, 3, chan_count)
    previous = from_behind(projected[-2:], "seq", 1)
    extended = jnp.concatenate([previous, projected], axis=0).astype(jnp.float32)
    short_mixed = (
        short_taps[0] * extended[2:]
        + short_taps[1] * extended[1:-1]
        + short_taps[2] * extended[:-2]
    )
    gate_out = short_mixed[:, 0]
    signal = short_mixed[:, 1] * short_mixed[:, 2]
    convolved = channel_convolve(signal, filter_taps)
    hidden = (gate_out * (convolved + skip_gain * signal)).astype(jnp.bfloat16)
    partial_terms = jnp.dot(hidden, out_weight, preferred_element_type=jnp.float32)
    layer_out = lax.psum_scatter(partial_terms, "chan", scatter_dimension=1, tiled=True)
    return layer_out.astype(jnp.bfloat16)


def solution(mesh):
    in_specs = (
        P("seq", "chan"),
        P(None, None, "chan"),
        P(None, None, "chan"),
        P("seq", "chan"),
        P("chan"),
        P("chan", None),
    )
    out_specs = P("seq", "chan")
    return jax.shard_map(body, mesh=mesh, in_specs=in_specs, out_specs=out_specs, check_vma=False)
```

profile of v0, /device:TPU:0, one launch (start us, length us, event | category | flops | bytes accessed | tf_op | source)
XLA Modules:
  0.0 442.7 jit_solution(17030054773035562507)
XLA Ops:
  7.3 8.7 %copy.70 = bf16[4096,3,256]{0,2,1:T(8,128)(2,1)} copy(bf16[4096,3,256]{2,0,1:T(8,128)(2,1)} %param.7) | data formatting | bytes 12582912 | tf_op args[1]
  16.0 74.3 %all-gather.2.cloned.1.call-done = bf16[1024,4096]{1,0:T(8,128)(2,1)} async-done(((bf16[1024,256]{1,0:T(8,128)(2,1)}), bf16[1024,4096]{1,0:T(8,128)(2,1)}) %all-gather.2.cloned.1.call-update) | async-done | bytes 8388624 | tf_op jit(solution)/shard_map/all_gather | solution.py:97
  90.3 11.0 %convolution_convert_fusion = bf16[1024,768]{1,0:T(8,128)(2,1)S(1)} fusion(bf16[1024,4096]{1,0:T(8,128)(2,1)} %all-gather.2.cloned.1.call-done, bf16[4096,768]{0,1:T(8,128)(2,1)} %bitcast.152), kind=kOutput, calls=%fused_computation.37 | convolution fusion | flops 6443237376 | bytes 16252928 | tf_op jit(solution)/shard_map/dot_general | solution.py:96
  102.6 3.4 collective-permute-start
  107.5 2.6 copy.71
  110.3 2.1 maximum_convert_fusion
  112.4 2.5 fusion.2
  116.6 2.9 copy.74
  119.5 4.8 %all-to-all-start = ((f32[2,1024,256]{1,0,2:T(2,128)}), f32[2,1024,256]{1,0,2:T(2,128)}, u32[]{:S(2)}, u32[]{:S(2)}) async-start(f32[2,1024,256]{1,0,2:T(2,128)} %copy.74), calls=%async_computation | async-start | bytes 4194304 | tf_op jit(solution)/shard_map/all_to_all | solution.py:63
  125.2 24.4 %all-to-all-done = f32[2,1024,256]{1,0,2:T(2,128)} async-done(((f32[2,1024,256]{1,0,2:T(2,128)}), f32[2,1024,256]{1,0,2:T(2,128)}, u32[]{:S(2)}, u32[]{:S(2)}) %all-to-all-start) | async-done | bytes 2097184 | tf_op jit(solution)/shard_map/all_to_all | solution.py:63
  149.6 3.6 copy.75
  153.2 2.9 copy.76
  156.1 6.2 %fusion.16 = f32[2,256,128,16]{2,3,1,0:T(8,128)S(1)} fusion(f32[2,8,256,128]{3,2,1,0:T(8,128)} %bitcast.149), kind=kOutput, calls=%fused_computation.32 | convolution fusion | flops 100665088 | bytes 6291456 | tf_op jit(solution)/shard_map/kn,xnmc->xkmc/dot_general | solution.py:29
  162.4 8.6 %fusion = (f32[2,16,256,128]{3,1,2,0:T(8,128)}, f32[2,16,256,128]{3,1,2,0:T(8,128)}) fusion(f32[2,256,128,16]{2,3,1,0:T(8,128)S(1)} %fusion.16, f32[16,256]{0,1:T(8,128)S(1)} %copy.80, f32[16,256]{0,1:T(8,128)S(1)} %copy.78, f32[2,8,256,128]{3,2,1,0:T(8,128)S(1)} %bitcast.150), kind=kOutput, calls=%fused_computation.2 | convolution fusion | flops 108005120 | bytes 14712832 | tf_op jit(solution)/shard_map/kn,xnmc->xkmc/dot_general | solution.py:28
  171.0 5.3 %copy.81 = f32[2,16,256,128]{2,3,1,0:T(8,128)} copy(f32[2,16,256,128]{3,1,2,0:T(8,128)} %get-tuple-element.5) | data formatting | bytes 8388608 | tf_op jit(solution)/shard_map/sub | solution.py:43
  176.3 5.3 %copy.82 = f32[2,16,256,128]{2,3,1,0:T(8,128)} copy(f32[2,16,256,128]{3,1,2,0:T(8,128)} %get-tuple-element.6) | data formatting | bytes 8388608 | tf_op jit(solution)/shard_map/add | solution.py:44
  181.6 7.6 %fusion.41 = f32[2,16,128,256]{3,2,1,0:T(8,128)S(1)} fusion(f32[2,16,256,128]{2,3,1,0:T(8,128)} %copy.82), kind=kOutput, calls=%fused_computation.62 | convolution fusion | flops 3222142976 | bytes 8388608 | tf_op jit(solution)/shard_map/kn,xanc->xakc/dot_general | solution.py:35
  189.2 4.6 %fusion.43 = f32[2,16,128,256]{3,2,1,0:T(8,128)S(1)} fusion(f32[2,16,256,128]{2,3,1,0:T(8,128)S(1)} %copy-done.1), kind=kOutput, calls=%fused_computation.64 | convolution fusion | flops 3222142976 | bytes 8388608 | tf_op jit(solution)/shard_map/kn,xanc->xakc/dot_general | solution.py:34
  193.9 4.7 %add_bitcast_fusion = f32[2,16,256,128]{2,3,1,0:T(8,128)S(1)} fusion(f32[2,16,128,256]{3,2,1,0:T(8,128)S(1)} %fusion.41, f32[2,16,256,128]{2,3,1,0:T(8,128)S(1)} %copy-done.1), kind=kOutput, calls=%fused_computation.6 | convolution fusion | flops 3224240128 | bytes 12582912 | tf_op jit(solution)/shard_map/kn,xanc->xakc/dot_general | solution.py:36
  198.6 5.0 %subtract_bitcast_fusion = f32[2,16,256,128]{2,3,1,0:T(8,128)S(1)} fusion(f32[2,16,128,256]{3,2,1,0:T(8,128)S(1)} %fusion.43, f32[2,16,256,128]{2,3,1,0:T(8,128)S(1)} %copy-done.2), kind=kOutput, calls=%fused_computation.7 | convolution fusion | flops 3224240128 | bytes 12582912 | tf_op jit(solution)/shard_map/kn,xanc->xakc/dot_general | solution.py:37
  204.6 2.8 fusion.8
  207.4 2.8 fusion.10
  210.2 2.9 fusion.20
  213.2 5.4 %fusion.7 = (f32[16,256,128]{1,2,0:T(8,128)}, f32[16,256,128]{1,2,0:T(8,128)}) fusion(f32[16,128,256]{2,1,0:T(8,128)S(1)} %fusion.20, f32[16,256]{1,0:T(8,128)S(1)} %get-tuple-element.14, f32[16,256]{1,0:T(8,128)S(1)} %get-tuple-element.15, f32[16,128,256]{2,1,0:T(8,128)S(1)} %fusion.8, f32[1,16,256,128]{2,3,1,0:T(8,128)S(1)} %get-tuple-element.7), kind=kOutput, calls=%fused_computation.19 | convolution fusion | flops 1615200256 | bytes 10518528 | tf_op jit(solution)/shard_map/kn,xanc->xakc/dot_general | solution.py:36
  218.6 3.0 copy.86
  221.6 3.1 copy.85
  224.7 3.0 fusion.75
  229.2 16.4 %all_to_all.34 = f32[2,1024,128]{2,1,0:T(8,128)} all-to-all(f32[2,1024,128]{2,1,0:T(8,128)S(1)} %bitcast.154), channel_id=1, replica_groups=mesh['seq'=2,'chan'=16] {'seq'}, dimensions={0} | all-to-all | bytes 2097152 | tf_op jit(solution)/shard_map/all_to_all | solution.py:89
  247.1 2.1 fusion.29
  249.2 8.1 %fusion.143 = f32[1024,4096]{1,0:T(8,128)} fusion(bf16[1024,256]{0,1:T(8,128)(2,1)S(1)} %fusion.29, bf16[256,4096]{1,0:T(8,128)(2,1)S(1)} %copy-done), kind=kOutput, calls=%fused_computation.161 | convolution fusion | flops 2147483648 | bytes 19398656 | tf_op jit(solution)/shard_map/dot_general | solution.py:113
  257.4 176.0 %reduce-scatter.2.cloned.1.call-done = f32[1024,256]{1,0:T(8,128)} async-done(((f32[1024,4096]{1,0:T(8,128)}), f32[1024,256]{1,0:T(8,128)}) %reduce-scatter.2.cloned.1.call-update) | async-done | bytes 1048592 | tf_op jit(solution)/shard_map/reduce_scatter | solution.py:114
  433.4 2.1 convert_element_type.67
  (38 shorter events, 10.2 us)
Async XLA Ops:
  6.5 242.7 %copy-start = (bf16[256,4096]{1,0:T(8,128)(2,1)S(1)}, bf16[256,4096]{1,0:T(8,128)(2,1)}, u32[]{:S(2)}) copy-start(bf16[256,4096]{1,0:T(8,128)(2,1)} %param.11) | copy-start | bytes 6291460
  6.5 83.8 %all-gather.2.cloned.1.call-start = ((), (), s32[]{:S(2)}) async-start(), calls=%async_computation.3 | async-start | bytes 8912896 | tf_op jit(solution)/shard_map/all_gather | solution.py:97
  90.3 15.6 %copy-start.7 = (f32[3,3,256]{2,1,0:T(4,128)S(1)}, f32[3,3,256]{2,1,0:T(4,128)}, u32[]{:S(2)}) copy-start(f32[3,3,256]{2,1,0:T(4,128)} %param.8) | copy-start | bytes 27652
  101.3 1.2 copy-start.6
  102.6 7.6 %collective-permute-start = (bf16[2,3,256]{2,1,0:T(4,128)(2,1)S(1)}, bf16[2,3,256]{2,1,0:T(4,128)(2,1)S(1)}, u32[]{:S(2)}, u32[]{:S(2)}) collective-permute-start(bf16[2,3,256]{2,1,0:T(4,128)(2,1)S(1)} %slice.51), channel_id=1, source_target_pairs={{0,16},{1,17},{2,18},{3,19},{4,20},{5,21},{6,22},{7,23},{8,24},{9,... | collective-permute-start | bytes 9224 | tf_op jit(solution)/shard_map/ppermute | solution.py:17
  114.9 1.6 copy-start.4
  119.5 30.2 %all-to-all-start = ((f32[2,1024,256]{1,0,2:T(2,128)}), f32[2,1024,256]{1,0,2:T(2,128)}, u32[]{:S(2)}, u32[]{:S(2)}) async-start(f32[2,1024,256]{1,0,2:T(2,128)} %copy.74), calls=%async_computation | async-start | bytes 4194304 | tf_op jit(solution)/shard_map/all_to_all | solution.py:63
  124.3 309.1 %reduce-scatter.2.cloned.1.call-start = ((), (), s32[]{:S(2)}) async-start(), calls=%async_computation.4 | async-start | bytes 17825792 | tf_op jit(solution)/shard_map/reduce_scatter | solution.py:114
  156.1 6.3 %copy-start.3 = (f32[2,2,1024,128]{3,2,1,0:T(8,128)S(1)}, f32[2,2,1024,128]{3,2,1,0:T(8,128)}, u32[]{:S(2)}) copy-start(f32[2,2,1024,128]{3,2,1,0:T(8,128)} %copy.76) | copy-start | bytes 6291460
  181.6 7.6 %copy-start.1 = (f32[2,16,256,128]{2,3,1,0:T(8,128)S(1)}, f32[2,16,256,128]{2,3,1,0:T(8,128)}, u32[]{:S(2)}) copy-start(f32[2,16,256,128]{2,3,1,0:T(8,128)} %copy.81) | copy-start | bytes 12582916
  193.9 4.8 %copy-start.2 = (f32[2,16,256,128]{2,3,1,0:T(8,128)S(1)}, f32[2,16,256,128]{2,3,1,0:T(8,128)}, u32[]{:S(2)}) copy-start(f32[2,16,256,128]{2,3,1,0:T(8,128)} %copy.82) | copy-start | bytes 12582916
  224.7 3.0 copy-start.5
  229.2 18.0 %copy-start.8 = (f32[256]{0:T(256)S(1)}, f32[256]{0:T(256)}, u32[]{:S(2)}) copy-start(f32[256]{0:T(256)} %param.10) | copy-start | bytes 3076
Sparse Core Ops, SparseCore 0:
  9.5 80.7 all-gather.1
  257.5 175.8 reduce-scatter.1
where the time goes:
time: 450 us; the launch traced here: 443 us
  waiting for transfers between devices  275 us (61%)
  matrix products  74.2 us (16%)
  local copies, waits for them, and re-layouts  43.6 us (10%)
  blocking collectives  16.4 us (4%)
  between operations  14.1 us (3%)
  other arithmetic  10.2 us (2%)
  starting transfers between devices  8.7 us (2%)
    reduce_scatter x1, waiting for transfers between devices, body(): lax.psum_scatter(partial_terms, 'chan', scatter_dimension=1, tiled=True)  176 us
    all_gather x1, waiting for transfers between devices, body(): lax.all_gather(tokens, 'chan', axis=1, tiled=True)  74.3 us
    all_to_all x1, waiting for transfers between devices, channel_convolve(): lax.all_to_all(stacked, 'seq', split_axis=2, concat_axis=1, tiled=True)  24.4 us
    all_to_all x1, blocking collectives, channel_convolve(): lax.all_to_all(values, 'seq', split_axis=0, concat_axis=1, tiled=True)  16.4 us
    unnamed x20, local copies, waits for them, and re-layouts  12.8 us
    dot_general x1, matrix products, body(): jnp.dot(lax.all_gather(tokens, 'chan', axis=1, tiled=True), flat_weight,...  11 us
    dot_general x2, matrix products, complex_transform(): cos_imag = jnp.einsum(pattern, cosine, imag_part, precision=highest)  10.5 us
    dot_general x2, matrix products, complex_transform(): sin_real = jnp.einsum(pattern, sines, real_part, precision=highest)  10.2 us
  transfers between devices with their start and end apart: 4, of which 3 were waited for; matrix products, arithmetic and copies ran while one was open for 3% of the time, Pallas kernels for 0%

commit v1 on v0

v1 whole, which is shorter than its diff:
```python
import functools
import math

import jax
import jax.numpy as jnp
import numpy as np
from jax import lax
from jax.experimental import pallas as pl
from jax.experimental.pallas import tpu as pltpu
from jax.sharding import PartitionSpec as P

MESH = pl.DeviceIdType.MESH
BF = jnp.bfloat16
F32 = jnp.float32
HALO = 16


def split_pair(array):
    high = array.astype(np.float32).astype(BF)
    low = (array - high.astype(np.float64)).astype(np.float32).astype(BF)
    return np.stack([np.asarray(high), np.asarray(low)])


def forward_matrix(block):
    angle = math.pi * (2 * np.arange(block)[:, None] + 1) * np.arange(block)[None, :] / (2 * block)
    return split_pair(np.concatenate([np.cos(angle), -np.sin(angle)], axis=0))


def inverse_matrix(block):
    place = block + np.arange(block)[:, None]
    angle = math.pi * place * (2 * np.arange(block)[None, :] + 1) / (2 * block)
    return split_pair(np.concatenate([np.cos(angle), -np.sin(angle)], axis=1) / block)


def dot(a, b):
    return jnp.dot(a, b, preferred_element_type=F32)


def remote(src, dst, send, recv, where):
    return pltpu.make_async_remote_copy(
        src_ref=src, dst_ref=dst, send_sem=send, recv_sem=recv, device_id=where, device_id_type=MESH
    )


def greet(devices):
    barrier = pltpu.get_barrier_semaphore()
    total = 0
    for where, exists in devices:
        if exists is None:
            pl.semaphore_signal(barrier, inc=1, device_id=where, device_id_type=MESH)
            total = total + 1
        else:

            @pl.when(exists)
            def _():
                pl.semaphore_signal(barrier, inc=1, device_id=where, device_id_type=MESH)

            total = total + exists.astype(jnp.int32)
    pl.semaphore_wait(barrier, total)


def position(chans):
    me = lax.axis_index("chan")
    far = chans // 4
    return me, me // 4, (me // 2) % 2, me % 2, far


def chan_peers(chans):
    me, zi, yi, ci, far = position(chans)
    core = {"chan": me + 1 - 2 * ci}
    side = {"chan": me + 2 - 4 * yi}
    up = {"chan": jnp.minimum(me + 4, chans - 1)}
    down = {"chan": jnp.maximum(me - 4, 0)}
    return core, side, up, down


def seq_peers(seqs):
    mine = lax.axis_index("seq")
    return mine, [{"seq": lax.rem(mine + k, seqs)} for k in range(1, seqs)]


def gather_kernel(
    seqs, chans, tok, weight, taps, fwd, proj, window,
    buf, acc, stage, whole, spec,
    zsend, zrecv, ysend, yrecv, csend, crecv, fsend, frecv,
):
    me, zi, yi, ci, far = position(chans)
    core, side, up, down = chan_peers(chans)
    mine, peers = seq_peers(seqs)
    rows, width = tok.shape
    narrow = taps.shape[1] // seqs
    block = fwd.shape[2]
    has_up, has_down = zi < far - 1, zi > 0
    greet([(core, None), (side, None), (up, has_up), (down, has_down)] + [(p, None) for p in peers])

    def send_up(src, z):
        return remote(src, buf.at[z * 4 + yi * 2 + ci], zsend.at[0, z], zrecv.at[z], up)

    def send_down(src, z):
        return remote(src, buf.at[z * 4 + yi * 2 + ci], zsend.at[1, z], zrecv.at[z], down)

    def send_side(src, z):
        return remote(src, buf.at[z * 4 + yi * 2 + ci], ysend.at[z], yrecv.at[z], side)

    def send_core(src, y, z):
        return remote(src, buf.at[z * 4 + y * 2 + ci], csend.at[y * far + z], crecv.at[y * far + z], core)

    def slot(z, y, c):
        return buf.at[z * 4 + y * 2 + c]

    def add(src, ident):
        part = weight[pl.ds(pl.multiple_of(ident * width, width), width), :]
        tile = min(rows, 256)

        @pl.loop(0, rows // tile)
        def _(r):
            at = pl.ds(pl.multiple_of(r * tile, tile), tile)
            acc[at, :] += dot(src[at, :], part)

    @pl.when(has_up)
    def _():
        send_up(tok, zi).start()

    @pl.when(has_down)
    def _():
        send_down(tok, zi).start()

    send_side(tok, zi).start()
    send_core(tok, yi, zi).start()

    for j in range(seqs):
        stage[j] = taps[:, j * narrow:(j + 1) * narrow]

    def filter_copy(k):
        to = lax.rem(mine + k, seqs)
        return remote(stage.at[to], whole.at[mine], fsend.at[k], frecv.at[k], {"seq": to})

    for k in range(1, seqs):
        filter_copy(k).start()
    whole[pl.ds(mine, 1)] = stage[pl.ds(mine, 1)]

    acc[...] = jnp.zeros_like(acc)
    add(tok, me)

    def from_side(z):
        here = slot(z, 1 - yi, ci)
        remote(here, here, ysend.at[z], yrecv.at[z], side).wait_recv()
        send_core(here, 1 - yi, z).start()
        add(here, z * 4 + (1 - yi) * 2 + ci)

    def from_core(y, z):
        here = slot(z, y, 1 - ci)
        remote(here, here, csend.at[y * far + z], crecv.at[y * far + z], core).wait_recv()
        add(here, z * 4 + y * 2 + 1 - ci)

    def far_in(z, going_up):
        here = slot(z, yi, ci)
        remote(here, here, zsend.at[0, z], zrecv.at[z], up).wait_recv()
        if going_up:

            @pl.when(has_up)
            def _():
                send_up(here, z).start()
        else:

            @pl.when(has_down)
            def _():
                send_down(here, z).start()

        send_side(here, z).start()
        send_core(here, yi, z).start()
        add(here, z * 4 + yi * 2 + ci)

    @pl.loop(1, far)
    def _(s):
        @pl.when(zi - s >= 0)
        def _():
            far_in(zi - s, True)

        @pl.when(zi + s < far)
        def _():
            far_in(zi + s, False)

        @pl.when(zi - s + 1 >= 0)
        def _():
            from_side(zi - s + 1)
            from_core(yi, zi - s + 1)

        @pl.when(jnp.logical_and(zi + s - 1 < far, s > 1))
        def _():
            from_side(zi + s - 1)
            from_core(yi, zi + s - 1)

    for k in range(1, seqs):
        came = lax.rem(mine - k + seqs, seqs)
        remote(stage.at[came], whole.at[came], fsend.at[k], frecv.at[k], {"seq": came}).wait_recv()
    per = rows // block
    count = seqs * per

    @pl.loop(0, count)
    def _(p):
        x = whole[p // per, pl.ds(pl.multiple_of((p % per) * block, block), block), :]
        high = x.astype(BF)
        low = (x - high.astype(F32)).astype(BF)
        spec[p] = dot(fwd[0], high) + (dot(fwd[0], low) + dot(fwd[1], high))

    parity = lax.broadcasted_iota(jnp.int32, (block, narrow), 0) % 2
    sign = (1 - 2 * parity).astype(F32)

    @pl.loop(0, count)
    def _(p):
        keep = jnp.where(p > 0, 1.0, 0.0).astype(F32)
        before = jnp.maximum(p - 1, 0)
        window[p, :block, :] = keep * spec[before, :block, :] + sign * spec[p, block:, :]
        window[p, block:, :] = keep * spec[before, block:, :] - sign * spec[p, :block, :]

    @pl.when(zi - far + 1 >= 0)
    def _():
        from_side(zi - far + 1)
        from_core(yi, zi - far + 1)

    @pl.when(zi + far - 1 < far)
    def _():
        from_side(zi + far - 1)
        from_core(yi, zi + far - 1)

    @pl.loop(0, far)
    def _(k):
        from_core(1 - yi, lax.rem(zi + k, far))

    proj[...] = acc[...].astype(BF)

    @pl.when(has_up)
    def _():
        @pl.loop(0, far)
        def _(z):
            @pl.when(z <= zi)
            def _():
                send_up(tok, z).wait_send()

    @pl.when(has_down)
    def _():
        @pl.loop(0, far)
        def _(z):
            @pl.when(z >= zi)
            def _():
                send_down(tok, z).wait_send()

    @pl.loop(0, far)
    def _(z):
        send_side(tok, z).wait_send()
        send_core(tok, 0, z).wait_send()
        send_core(tok, 1, z).wait_send()

    for k in range(1, seqs):
        filter_copy(k).wait_send()


def mix_kernel(
    seqs, proj, short, skip, fwd, inv, window, hidden,
    ext, edge, signal, gate, stage, whole, spec, prod, back, done,
    hsend, hrecv, ssend, srecv, bsend, brecv,
):
    mine, peers = seq_peers(seqs)
    rows = proj.shape[0]
    chan = proj.shape[1] // 3
    narrow = chan // seqs
    block = fwd.shape[2]
    per = rows // block
    count = seqs * per
    greet([(p, None) for p in peers])
    has_next, has_before = mine < seqs - 1, mine > 0
    following = {"seq": jnp.minimum(mine + 1, seqs - 1)}
    halo = remote(proj.at[pl.ds(rows - HALO, HALO)], edge, hsend, hrecv, following)

    @pl.when(has_next)
    def _():
        halo.start()

    ext[HALO:, :] = proj[...].astype(F32)

    @pl.when(has_before)
    def _():
        halo.wait_recv()
        ext[:HALO, :] = edge[...].astype(F32)

    @pl.when(jnp.logical_not(has_before))
    def _():
        ext[:HALO, :] = jnp.zeros((HALO, 3 * chan), F32)

    tile = min(rows, 128)
    for r in range(rows // tile):
        at = HALO + r * tile

        def mixed(g):
            cols = slice(g * chan, (g + 1) * chan)
            return (
                short[g:g + 1, :] * ext[at:at + tile, cols]
                + short[3 + g:4 + g, :] * ext[at - 1:at - 1 + tile, cols]
                + short[6 + g:7 + g, :] * ext[at - 2:at - 2 + tile, cols]
            )

        gate[r * tile:(r + 1) * tile, :] = mixed(0)
        value = mixed(1) * mixed(2)
        signal[r * tile:(r + 1) * tile, :] = value
        for j in range(seqs):
            stage[j, r * tile:(r + 1) * tile, :] = value[:, j * narrow:(j + 1) * narrow].astype(BF)

    def signal_copy(k):
        to = lax.rem(mine + k, seqs)
        return remote(stage.at[to], whole.at[mine], ssend.at[k], srecv.at[k], {"seq": to})

    for k in range(1, seqs):
        signal_copy(k).start()
    whole[pl.ds(mine, 1)] = stage[pl.ds(mine, 1)]

    def transform(owner):
        @pl.loop(0, per)
        def _(q):
            x = whole[owner, pl.ds(pl.multiple_of(q * block, block), block), :]
            spec[owner * per + q] = dot(fwd[0], x) + dot(fwd[1], x)

    transform(mine)
    for k in range(1, seqs):
        came = lax.rem(mine - k + seqs, seqs)
        remote(stage.at[came], whole.at[came], ssend.at[k], srecv.at[k], {"seq": came}).wait_recv()
        transform(came)

    @pl.loop(0, block // 8)
    def _(r):
        real = pl.ds(pl.multiple_of(r * 8, 8), 8)
        imag = pl.ds(pl.multiple_of(block + r * 8, 8), 8)
        for k in range(count):
            re = im = None
            for j in range(k + 1):
                a, b = spec[j, real, :], spec[j, imag, :]
                c, d = window[k - j, real, :], window[k - j, imag, :]
                one, two = a * c - b * d, a * d + b * c
                re = one if re is None else re + one
                im = two if im is None else im + two
            prod[k, real, :] = re
            prod[k, imag, :] = im

    def invert(owner):
        @pl.loop(0, per)
        def _(q):
            x = prod[owner * per + q]
            high = x.astype(BF)
            low = (x - high.astype(F32)).astype(BF)
            y = dot(inv[0], high) + (dot(inv[0], low) + dot(inv[1], high))
            back[owner, pl.ds(pl.multiple_of(q * block, block), block), :] = y.astype(BF)

    def back_copy(k):
        to = lax.rem(mine + k, seqs)
        return remote(back.at[to], done.at[mine], bsend.at[k], brecv.at[k], {"seq": to})

    for k in range(1, seqs):
        invert(lax.rem(mine + k, seqs))
        back_copy(k).start()
    invert(mine)
    done[pl.ds(mine, 1)] = back[pl.ds(mine, 1)]
    for k in range(1, seqs):
        came = lax.rem(mine - k + seqs, seqs)
        remote(back.at[came], done.at[came], bsend.at[k], brecv.at[k], {"seq": came}).wait_recv()

    for j in range(seqs):
        cols = slice(j * narrow, (j + 1) * narrow)
        for r in range(rows // tile):
            at = slice(r * tile, (r + 1) * tile)
            conv = done[j, at, :].astype(F32)
            hidden[at, cols] = (
                gate[at, cols] * (conv + skip[:, cols] * signal[at, cols])
            ).astype(BF)

    for k in range(1, seqs):
        signal_copy(k).wait_send()
        back_copy(k).wait_send()

    @pl.when(has_next)
    def _():
        halo.wait_send()


def scatter_kernel(
    chans, hidden, weight, out,
    cout, cin, yout, yin, zout, upin, downin,
    csend, crecv, ysend, yrecv, zsend, urecv, drecv,
):
    me, zi, yi, ci, far = position(chans)
    core, side, up, down = chan_peers(chans)
    rows, width = out.shape
    has_up, has_down = zi < far - 1, zi > 0
    greet([(core, None), (side, None), (up, has_up), (down, has_down)])

    tile = min(rows, 256)
    tiles = rows // tile

    def term(z, y, c, at):
        ident = z * 4 + y * 2 + c
        cols = pl.ds(pl.multiple_of(ident * width, width), width)
        return dot(hidden[at, :], weight[:, cols])

    def each_tile(do):
        @pl.loop(0, tiles)
        def _(r):
            do(pl.ds(pl.multiple_of(r * tile, tile), tile))

    def core_copy(y, z):
        return remote(cout.at[y * far + z], cin.at[y * far + z], csend.at[y * far + z], crecv.at[y * far + z], core)

    def side_copy(z):
        return remote(yout.at[z], yin.at[z], ysend.at[z], yrecv.at[z], side)

    def up_copy(z):
        return remote(zout.at[z], upin.at[z], zsend.at[z], urecv.at[z], up)

    def down_copy(z):
        return remote(zout.at[z], downin.at[z], zsend.at[z], drecv.at[z], down)

    def far_first(do):
        @pl.loop(0, far)
        def _(s):
            d = far - 1 - s

            @pl.when(zi + d < far)
            def _():
                do(zi + d)

            @pl.when(jnp.logical_and(zi - d >= 0, d > 0))
            def _():
                do(zi - d)

    def to_core(y):
        def go(z):
            def tiled(at):
                cout[y * far + z, at, :] = term(z, y, 1 - ci, at).astype(BF)

            each_tile(tiled)
            core_copy(y, z).start()

        return go

    def to_side(z):
        core_copy(1 - yi, z).wait_recv()

        def tiled(at):
            total = term(z, 1 - yi, ci, at) + cin[(1 - yi) * far + z, at, :].astype(F32)
            yout[z, at, :] = total.astype(BF)

        each_tile(tiled)
        side_copy(z).start()

    def total(z, at):
        return (
            term(z, yi, ci, at)
            + cin[yi * far + z, at, :].astype(F32)
            + yin[z, at, :].astype(F32)
        )

    def pass_on(z, arrived, land, copy, onward):
        core_copy(yi, z).wait_recv()
        side_copy(z).wait_recv()

        @pl.when(arrived)
        def _():
            onward(z).wait_recv()

            def tiled(at):
                zout[z, at, :] = (total(z, at) + land[z, at, :].astype(F32)).astype(BF)

            each_tile(tiled)

        @pl.when(jnp.logical_not(arrived))
        def _():
            def tiled(at):
                zout[z, at, :] = total(z, at).astype(BF)

            each_tile(tiled)

        copy(z).start()

    far_first(to_core(1 - yi))
    far_first(to_side)
    far_first(to_core(yi))

    @pl.loop(0, far - 1)
    def _(s):
        d = far - 1 - s

        @pl.when(zi + d < far)
        def _():
            pass_on(zi + d, has_down, upin, up_copy, up_copy)

        @pl.when(zi - d >= 0)
        def _():
            pass_on(zi - d, has_up, downin, down_copy, down_copy)

    core_copy(yi, zi).wait_recv()
    side_copy(zi).wait_recv()

    @pl.when(has_down)
    def _():
        up_copy(zi).wait_recv()

    @pl.when(has_up)
    def _():
        down_copy(zi).wait_recv()

    def finish(at):
        whole = total(zi, at)
        both = jnp.logical_and(has_down, has_up)

        @pl.when(both)
        def _():
            out[at, :] = (whole + upin[zi, at, :].astype(F32) + downin[zi, at, :].astype(F32)).astype(BF)

        @pl.when(jnp.logical_and(has_down, jnp.logical_not(has_up)))
        def _():
            out[at, :] = (whole + upin[zi, at, :].astype(F32)).astype(BF)

        @pl.when(jnp.logical_and(has_up, jnp.logical_not(has_down)))
        def _():
            out[at, :] = (whole + downin[zi, at, :].astype(F32)).astype(BF)

    each_tile(finish)

    @pl.loop(0, far)
    def _(z):
        core_copy(0, z).wait_send()
        core_copy(1, z).wait_send()
        side_copy(z).wait_send()

        @pl.when(z > zi)
        def _():
            up_copy(z).wait_send()

        @pl.when(z < zi)
        def _():
            down_copy(z).wait_send()


def call(kernel, out_shape, arity, scratch, ident):
    vmem = pl.BlockSpec(memory_space=pltpu.VMEM)
    many = isinstance(out_shape, (list, tuple))
    return pl.pallas_call(
        kernel,
        out_shape=out_shape,
        in_specs=[vmem] * arity,
        out_specs=[vmem] * len(out_shape) if many else vmem,
        scratch_shapes=scratch,
        compiler_params=pltpu.CompilerParams(
            collective_id=ident, has_side_effects=True, vmem_limit_bytes=50 * 2**20
        ),
    )


def body(seqs, chans, tokens, in_weight, short_taps, filter_taps, skip_gain, out_weight):
    rows, width = tokens.shape
    chan = in_weight.shape[2]
    far = chans // 4
    block = min(256, rows)
    count = seqs * rows // block
    narrow = chan // seqs
    dma = pltpu.SemaphoreType.DMA
    vm = pltpu.VMEM
    shape = jax.ShapeDtypeStruct
    flat_weight = in_weight.reshape(in_weight.shape[0], 3 * chan)
    fwd = jnp.asarray(forward_matrix(block))
    inv = jnp.asarray(inverse_matrix(block))
    projected, window = call(
        functools.partial(gather_kernel, seqs, chans),
        [shape((rows, 3 * chan), BF), shape((count, 2 * block, narrow), F32)],
        4,
        [
            vm((chans, rows, width), BF), vm((rows, 3 * chan), F32),
            vm((seqs, rows, narrow), F32), vm((seqs, rows, narrow), F32),
            vm((count, 2 * block, narrow), F32),
            dma((2, far)), dma((far,)), dma((far,)), dma((far,)),
            dma((2 * far,)), dma((2 * far,)), dma((seqs,)), dma((seqs,)),
        ],
        0,
    )(tokens, flat_weight, filter_taps, fwd)
    hidden = call(
        functools.partial(mix_kernel, seqs),
        shape((rows, chan), BF),
        6,
        [
            vm((HALO + rows, 3 * chan), F32), vm((HALO, 3 * chan), BF),
            vm((rows, chan), F32), vm((rows, chan), F32),
            vm((seqs, rows, narrow), BF), vm((seqs, rows, narrow), BF),
            vm((count, 2 * block, narrow), F32), vm((count, 2 * block, narrow), F32),
            vm((seqs, rows, narrow), BF), vm((seqs, rows, narrow), BF),
            dma, dma, dma((seqs,)), dma((seqs,)), dma((seqs,)), dma((seqs,)),
        ],
        1,
    )(projected, short_taps.reshape(9, chan), skip_gain.reshape(1, chan), fwd, inv, window)
    return call(
        functools.partial(scatter_kernel, chans),
        shape((rows, width), BF),
        2,
        [
            vm((2 * far, rows, width), BF), vm((2 * far, rows, width), BF),
            vm((far, rows, width), BF), vm((far, rows, width), BF),
            vm((far, rows, width), BF), vm((far, rows, width), BF), vm((far, rows, width), BF),
            dma((2 * far,)), dma((2 * far,)), dma((far,)), dma((far,)),
            dma((far,)), dma((far,)), dma((far,)),
        ],
        2,
    )(hidden, out_weight)


def solution(mesh):
    in_specs = (
        P("seq", "chan"),
        P(None, None, "chan"),
        P(None, None, "chan"),
        P("seq", "chan"),
        P("chan"),
        P("chan", None),
    )
    out_specs = P("seq", "chan")
    run = functools.partial(body, mesh.shape["seq"], mesh.shape["chan"])
    return jax.shard_map(run, mesh=mesh, in_specs=in_specs, out_specs=out_specs, check_vma=False)
```

time: 450 us -> 165 us (0.37); the launches traced: 443 us -> 164 us
  waiting for transfers between devices: 275 us -> 0 us
  Pallas kernels: 0 us -> 141 us
  matrix products: 74.2 us -> 0 us
  local copies, waits for them, and re-layouts: 43.6 us -> 23 us
  blocking collectives: 16.4 us -> 0 us
  between operations: 14.1 us -> 0.07 us
  other arithmetic: 10.2 us -> 0 us
  starting transfers between devices: 8.7 us -> 0 us
    reduce_scatter x1 -> x0, waiting for transfers between devices: 176 us -> none  [body(): lax.psum_scatter(partial_terms, 'chan', scatter_dimension=1, tiled=True)]
    pallas_call x0 -> x3, Pallas kernels: none -> 141 us  [the longest x1 64.1 us: body(): call(functools.partial(gather_kernel, seqs, chans), [shape((rows, 3 * cha...]
    all_gather x1 -> x0, waiting for transfers between devices: 74.3 us -> none  [body(): lax.all_gather(tokens, 'chan', axis=1, tiled=True)]
    dot_general x14 -> x0, matrix products: 74.2 us -> none  [the longest x1 11 us: body(): jnp.dot(lax.all_gather(tokens, 'chan', axis=1, tiled=True), flat_weight,...]
    all_to_all x1 -> x0, waiting for transfers between devices: 24.4 us -> none  [channel_convolve(): lax.all_to_all(stacked, 'seq', split_axis=2, concat_axis=1, tiled=True)]
    all_to_all x1 -> x0, blocking collectives: 16.4 us -> none  [channel_convolve(): lax.all_to_all(values, 'seq', split_axis=0, concat_axis=1, tiled=True)]
    another operation x3 -> x0, local copies, waits for them, and re-layouts: 9.04 us -> none
    reshape x0 -> x2, local copies, waits for them, and re-layouts: none -> 8.72 us  [the longest x1 8.71 us: body(): flat_weight = in_weight.reshape(in_weight.shape[0], 3 * chan)]
  transfers between devices with their start and end apart: 4 -> 0, of which waited for: 3 -> 0; matrix products, arithmetic and copies ran while one was open for 3% -> 0% of each run, Pallas kernels for 0% -> 0%
where the time goes in v1:
time: 165 us; the launch traced here: 164 us
  Pallas kernels  141 us (85%)
  local copies, waits for them, and re-layouts  23 us (14%)
    pallas_call x1, Pallas kernels, body(): call(functools.partial(gather_kernel, seqs, chans), [shape((rows, 3 * cha...  64.1 us
    pallas_call x1, Pallas kernels, body(): call(functools.partial(scatter_kernel, chans), shape((rows, width), BF),...  55.9 us
    pallas_call x1, Pallas kernels, body(): call(functools.partial(mix_kernel, seqs), shape((rows, chan), BF), 6, [vm...  20.9 us
    unnamed x20, local copies, waits for them, and re-layouts  14.3 us
    reshape x1, local copies, waits for them, and re-layouts, body(): flat_weight = in_weight.reshape(in_weight.shape[0], 3 * chan)  8.71 us

profile of v1, /device:TPU:0, one launch (start us, length us, event | category | flops | bytes accessed | tf_op | source)
XLA Modules:
  0.0 164.0 jit_solution(3149937908617633258)
XLA Ops:
  0.0 8.7 %copy.10 = bf16[4096,3,256]{0,2,1:T(8,128)(2,1)} copy(bf16[4096,3,256]{2,0,1:T(8,128)(2,1)} %param.9) | data formatting | bytes 12582912 | tf_op args[1]
  8.7 0.0 copy-start
  8.7 0.0 copy-start.5
  8.7 8.7 %copy.11.weight = bf16[4096,768]{1,0:T(8,128)(2,1)} copy(bf16[4096,768]{0,1:T(8,128)(2,1)} %bitcast.3) | data formatting | bytes 12582912 | tf_op jit(solution)/shard_map/reshape | solution.py:567
  17.4 0.0 copy-done
  17.4 0.0 copy-done.5
  17.4 0.0 copy-start.4
  17.4 1.2 copy-done.4
  18.7 0.0 copy-start.8
  18.7 0.0 copy-start.7
  18.7 0.0 copy-start.1
  18.7 64.1 %shard_map.82 = (bf16[1024,768]{1,0:T(8,128)(2,1)S(1)}, f32[8,512,128]{2,1,0:T(8,128)}) custom-call(bf16[1024,256]{1,0:T(8,128)(2,1)S(1)} %copy-done.5, bf16[4096,768]{1,0:T(8,128)(2,1)} %copy.11.weight, f32[1024,256]{1,0:T(8,128)S(1)} %copy-done.4, bf16[2,512,256]{2,1,0:T(8,128)(2,1)S(1)} %copy-done), custom_call_target="tpu_custom_call" | custom-call | tf_op jit(solution)/shard_map/pallas_call | solution.py:570
  82.7 0.0 copy-start.2
  82.8 1.1 copy-done.2
  83.9 0.0 copy-done.8
  83.9 0.0 copy-done.7
  83.9 0.0 copy-start.3
  83.9 1.4 copy-done.3
  85.3 0.0 copy-start.6
  85.3 1.0 copy-done.6
  86.4 20.9 %shard_map.83.hidden = bf16[1024,256]{1,0:T(8,128)(2,1)S(1)} custom-call(bf16[1024,768]{1,0:T(8,128)(2,1)S(1)} %copy-done.3, f32[9,256]{1,0:T(8,128)S(1)} %reshape.10.short, f32[1,256]{1,0:T(1,128)S(1)} %bitcast.2, bf16[2,512,256]{2,1,0:T(8,128)(2,1)S(1)} %copy-done, bf16[2,256,512]{2,1,0:T(8,128)(2,1)S(1)} %copy-done.6, f32[8,512,128]{2,1,0:T(8,128)} %get-tuple-element.8.window), custom_call_target="tpu_custom_call" | custom-call | tf_op jit(solution)/shard_map/pallas_call | solution.py:583
  107.3 0.0 copy-done.1
  107.3 55.9 %shard_map.84 = bf16[1024,256]{1,0:T(8,128)(2,1)S(1)} custom-call(bf16[1024,256]{1,0:T(8,128)(2,1)S(1)} %shard_map.83.hidden, bf16[256,4096]{1,0:T(8,128)(2,1)S(1)} %copy-done.1), custom_call_target="tpu_custom_call" | custom-call | tf_op jit(solution)/shard_map/pallas_call | solution.py:597
  163.2 0.8 copy.13
  (1 shorter events, 0.0 us)
Async XLA Ops:
  8.7 8.7 %copy-start = (bf16[2,512,256]{2,1,0:T(8,128)(2,1)S(1)}, bf16[2,512,256]{2,1,0:T(8,128)(2,1)}, u32[]{:S(2)}) copy-start(bf16[2,512,256]{2,1,0:T(8,128)(2,1)} %constant.4.clone.fwd) | copy-start | bytes 1572868
  8.7 8.7 %copy-start.5 = (bf16[1024,256]{1,0:T(8,128)(2,1)S(1)}, bf16[1024,256]{1,0:T(8,128)(2,1)}, u32[]{:S(2)}) copy-start(bf16[1024,256]{1,0:T(8,128)(2,1)} %tok.1) | copy-start | bytes 1572868
  17.4 1.2 copy-start.4
  18.7 65.2 %copy-start.8 = (f32[3,3,256]{2,1,0:T(4,128)S(1)}, f32[3,3,256]{2,1,0:T(4,128)}, u32[]{:S(2)}) copy-start(f32[3,3,256]{2,1,0:T(4,128)} %param.10) | copy-start | bytes 27652
  18.7 65.2 %copy-start.7 = (f32[256]{0:T(256)S(1)}, f32[256]{0:T(256)}, u32[]{:S(2)}) copy-start(f32[256]{0:T(256)} %param.12) | copy-start | bytes 3076
  18.7 88.6 %copy-start.1 = (bf16[256,4096]{1,0:T(8,128)(2,1)S(1)}, bf16[256,4096]{1,0:T(8,128)(2,1)}, u32[]{:S(2)}) copy-start(bf16[256,4096]{1,0:T(8,128)(2,1)} %weight.1) | copy-start | bytes 6291460
  82.7 1.1 copy-start.2
  83.9 1.4 copy-start.3
  85.3 1.0 copy-start.6
